TPU v7x, 32 devices: a whole 2x2x4 slice. The times are simulated.
32 devices in a mesh: runs: 2 (over x), tm: 8 (over z, y), hyd: 2 (over core).
Axes of the slice: x: 2, y: 2, z: 4, core: 2. Of those that a mesh axis runs over, the one named last changes fastest.
Arguments:
- record: bfloat16 [524160, 1024], P(('runs', 'tm'), 'hyd'), parts along dimension 0, may hold values from -6 to 6
- chips: int32 [4095], replicated, may hold values from -1 to 1, as said below
- steer_lags: int32 [1024, 256], P('hyd'), may hold values from 0 to 7
Outputs:
- power: float32 [128, 512, 256], P('runs', 'tm', 'hyd'), parts along dimension 0
There are 2 independent parts, one for each index of `runs`. A program takes and returns all parts, laid end to end along the dimension named above; an argument that names none is the same for every part. Nothing has to cross between parts.
Inputs may be any that keep to these rules, and one draw needn't show every extreme that they name: The chips are +1 or -1 and form one period of a maximal-length sequence of period 4095, starting at a drawn phase.
All inputs are finite; a program needn't handle non-finite values.
Results may differ from a plain program's by a relative error of at most 0.0047.
Values may be sent and summed in bfloat16 or wider, within the bound.
A program may use at most 256 MiB of HBM per device.

v0:
```python
import math
import jax
import jax.numpy as jnp
from jax import lax
from jax.sharding import PartitionSpec as P

CODE = 4095
HYDRO = 1024
DELAYS = 512
PERIODS = 64
BEAMS = 256
MAXLAG = 8


def passed_along(array, axis, by):
    length = lax.axis_size(axis)
    pairs = [(i, i + by) for i in range(length) if 0 <= i + by < length]
    return lax.ppermute(array, axis, pairs)


def toeplitz_code(chips):
    seg_len = CODE + DELAYS - 1
    padded = jnp.concatenate([chips.astype(jnp.float32), jnp.zeros((DELAYS,), jnp.float32)])
    tiled = jnp.tile(padded, DELAYS)[: DELAYS * seg_len]
    return tiled.reshape(DELAYS, seg_len).astype(jnp.bfloat16)


def dft_table(length):
    freq = jnp.arange(length, dtype=jnp.int32)
    phase = (freq[:, None] * freq[None, :] % length).astype(jnp.float32) * (2.0 * math.pi / length)
    weight = 1.0 / math.sqrt(length)
    return jnp.concatenate([jnp.cos(phase) * weight, -jnp.sin(phase) * weight], 0).astype(
        jnp.bfloat16
    )


def body(record, chips, steer_lags):
    hyd_local = record.shape[1]
    tm_size = lax.axis_size("tm")
    local_periods = PERIODS // tm_size
    delay_rows = DELAYS // tm_size
    seg_len = CODE + DELAYS - 1
    norm_code = 1.0 / math.sqrt(CODE)
    tail_rows = passed_along(record[: DELAYS - 1], "tm", -1)
    extended = jnp.concatenate([record, tail_rows], 0)
    toeplitz = toeplitz_code(chips)
    profile_list = []
    for period in range(local_periods):
        segment = extended[period * CODE : period * CODE + seg_len]
        profile_list.append(
            (jnp.dot(toeplitz, segment, preferred_element_type=jnp.float32) * norm_code).astype(
                jnp.bfloat16
            )
        )
    profiles = jnp.stack(profile_list, 0)
    transform = dft_table(PERIODS)
    received = lax.all_to_all(profiles, "tm", split_axis=1, concat_axis=0, tiled=True)
    trailing = received.shape[1:]
    flattened = received.reshape(received.shape[0], -1)
    spectral = jnp.dot(transform, flattened, preferred_element_type=jnp.float32).astype(
        jnp.bfloat16
    )
    spectrum = spectral.reshape((2, received.shape[0]) + trailing)
    next_rows = passed_along(spectrum[:, :, : MAXLAG - 1, :], "tm", -1)
    spec_ext = jnp.concatenate([spectrum, next_rows], 2)
    norm_hydro = 1.0 / math.sqrt(HYDRO)
    shifted_list = [
        spec_ext[:, :, offset : offset + delay_rows, :].reshape(2 * PERIODS * delay_rows, hyd_local)
        for offset in range(MAXLAG)
    ]
    beam_local = BEAMS // lax.axis_size("hyd")
    partial_sum = jnp.zeros((2 * PERIODS * delay_rows, BEAMS), jnp.float32)
    for offset in range(MAXLAG):
        selector = (steer_lags == offset).astype(jnp.bfloat16)
        partial_sum = partial_sum + jnp.dot(
            shifted_list[offset], selector, preferred_element_type=jnp.float32
        )
    summed = lax.psum(partial_sum * norm_hydro, "hyd")
    owned = lax.dynamic_slice_in_dim(summed, lax.axis_index("hyd") * beam_local, beam_local, 1)
    owned = owned.reshape(2, PERIODS, delay_rows, beam_local)
    return owned[0] * owned[0] + owned[1] * owned[1]


def solution(mesh):
    in_specs = (P(("runs", "tm"), "hyd"), P(), P("hyd", None))
    out_specs = P("runs", "tm", "hyd")
    return jax.shard_map(body, mesh=mesh, in_specs=in_specs, out_specs=out_specs, check_vma=False)
```

profile of v0, /device:TPU:0, one launch (start us, length us, event | category | flops | bytes accessed | tf_op | source)
XLA Modules:
  0.0 408.6 jit_solution(9783359401931948476)
XLA Ops:
  12.1 11.8 %tile.11 = bf16[2358784]{0:T(1024)(128)(2,1)} reshape(bf16[512,4607]{1,0:T(8,128)(2,1)} %tile.10) | data formatting | bytes 9435136 | tf_op jit(solution)/shard_map/tile | solution.py:24
  23.9 5.7 %slice.85 = bf16[2358272]{0:T(1024)(128)(2,1)} slice(bf16[2358784]{0:T(1024)(128)(2,1)} %tile.11), slice={[0:2358272]} | slice | bytes 9433088 | tf_op jit(solution)/shard_map/slice | solution.py:24
  29.6 11.3 %convert_element_type.50 = bf16[512,4606]{1,0:T(8,128)(2,1)} reshape(bf16[2358272]{0:T(1024)(128)(2,1)} %slice.85) | data formatting | bytes 9433088 | tf_op jit(solution)/shard_map/convert_element_type | solution.py:25
  40.9 7.3 %fusion.65 = bf16[8,512,512]{2,1,0:T(8,128)(2,1)} fusion(bf16[512,4606]{1,0:T(8,128)(2,1)} %convert_element_type.50, bf16[32760,512]{1,0:T(8,128)(2,1)} %param.3), kind=kOutput, calls=%fused_computation.47 | convolution fusion | flops 2415394816 | bytes 9961472 | tf_op jit(solution)/shard_map/dot_general | solution.py:51
  48.3 5.9 %fusion.73 = bf16[8,512,512]{2,1,0:T(8,128)(2,1)} fusion(bf16[8,512,512]{2,1,0:T(8,128)(2,1)} %fusion.65, bf16[512,4606]{1,0:T(8,128)(2,1)S(1)} %copy-done.1, bf16[32760,512]{1,0:T(8,128)(2,1)} %param.3), kind=kOutput, calls=%fused_computation.51 | convolution fusion | flops 2415394816 | bytes 9959424 | tf_op jit(solution)/shard_map/dot_general | solution.py:51
  54.2 6.6 %fusion.79 = bf16[8,512,512]{2,1,0:T(8,128)(2,1)} fusion(bf16[8,512,512]{2,1,0:T(8,128)(2,1)} %fusion.73, bf16[512,4606]{1,0:T(8,128)(2,1)S(1)} %copy-done.1, bf16[32760,512]{1,0:T(8,128)(2,1)} %param.3), kind=kOutput, calls=%fused_computation.53 | convolution fusion | flops 2415394816 | bytes 9959424 | tf_op jit(solution)/shard_map/dot_general | solution.py:51
  76.5 5.9 %fusion.69 = bf16[8,512,512]{2,1,0:T(8,128)(2,1)} fusion(bf16[8,512,512]{2,1,0:T(8,128)(2,1)} %fusion.103, bf16[512,4606]{1,0:T(8,128)(2,1)} %convert_element_type.50, bf16[511,512]{1,0:T(8,128)(2,1)S(1)} %collective-permute-done, bf16[32760,512]{1,0:T(8,128)(2,1)S(1)} %bitcast.82), kind=kOutput, calls=%fused_computation.49 | convolution fusion | flops 2424827904 | bytes 39312384 | tf_op jit(solution)/shard_map/dot_general | solution.py:51
  82.5 6.9 %copy.5 = bf16[8,512,512]{2,0,1:T(8,128)(2,1)} copy(bf16[8,512,512]{2,1,0:T(8,128)(2,1)} %fusion.69) | data formatting | bytes 8388608 | tf_op jit(solution)/shard_map/stack | solution.py:55
  89.3 8.4 %all-to-all-start = ((bf16[8,512,512]{2,0,1:T(8,128)(2,1)}), bf16[8,512,512]{2,0,1:T(8,128)(2,1)}, u32[]{:S(2)}, u32[]{:S(2)}) async-start(bf16[8,512,512]{2,0,1:T(8,128)(2,1)} %copy.5), calls=%async_computation | async-start | bytes 8388608 | tf_op jit(solution)/shard_map/all_to_all | solution.py:57
  98.0 92.8 %all-to-all-done = bf16[8,512,512]{2,0,1:T(8,128)(2,1)} async-done(((bf16[8,512,512]{2,0,1:T(8,128)(2,1)}), bf16[8,512,512]{2,0,1:T(8,128)(2,1)}, u32[]{:S(2)}, u32[]{:S(2)}) %all-to-all-start) | async-done | bytes 4194336 | tf_op jit(solution)/shard_map/all_to_all | solution.py:57
  197.1 5.6 %convolution_convert_fusion = bf16[128,32768]{1,0:T(8,128)(2,1)} fusion(bf16[64,32768]{1,0:T(8,128)(2,1)S(1)} %bitcast.83, bf16[64,64]{1,0:T(8,128)(2,1)S(1)} %get-tuple-element.12, bf16[64,64]{1,0:T(8,128)(2,1)S(1)} %get-tuple-element.13), kind=kOutput, calls=%fused_computation | convolution fusion | flops 541097984 | bytes 12599296 | tf_op jit(solution)/shard_map/dot_general | solution.py:60
  202.7 13.6 %reshape_reshape.3 = bf16[8192,512]{1,0:T(8,128)(2,1)} reshape(bf16[128,32768]{1,0:T(8,128)(2,1)} %convolution_convert_fusion) | data formatting | bytes 16777216 | tf_op jit(solution)/shard_map/reshape;reshape | solution.py:68
  216.3 10.2 %copy.11 = bf16[16,8,64,512]{3,2,1,0:T(8,128)(2,1)} copy(bf16[16,8,64,512]{3,1,2,0:T(8,128)(2,1)} %bitcast.69) | data formatting | bytes 16777216
  226.6 8.0 %constant_dynamic-update-slice_fusion = bf16[2,64,71,512]{3,2,1,0:T(8,128)(2,1)} fusion(bf16[2,64,64,512]{3,2,1,0:T(8,128)(2,1)} %bitcast.79), kind=kLoop, calls=%fused_computation.94 | loop fusion | bytes 16777216
  237.5 9.1 %fusion.113 = f32[8192,256]{1,0:T(8,128)} fusion(bf16[8192,512]{1,0:T(8,128)(2,1)} %reshape_reshape.3, s32[512,256]{1,0:T(8,128)S(1)} %copy-done), kind=kOutput, calls=%fused_computation.70 | convolution fusion | flops 2147614720 | bytes 17301504 | tf_op jit(solution)/shard_map/dot_general | solution.py:75
  246.7 12.5 %collective-permute-done.1 = bf16[2,64,7,512]{3,1,2,0:T(8,128)(2,1)S(1)} collective-permute-done((bf16[2,64,7,512]{3,1,2,0:T(8,128)(2,1)S(1)}, bf16[2,64,7,512]{3,1,2,0:T(8,128)(2,1)S(1)}, u32[]{:S(2)}, u32[]{:S(2)}) %collective-permute-start.1) | collective-permute-done | bytes 917536 | tf_op jit(solution)/shard_map/ppermute | solution.py:18
  260.7 52.8 %fusion.142 = (bf16[2,64,64,512]{3,2,1,0:T(8,128)(2,1)}, bf16[2,64,64,512]{3,2,1,0:T(8,128)(2,1)}, bf16[2,64,64,512]{3,2,1,0:T(8,128)(2,1)}, bf16[2,64,64,512]{3...) fusion(bf16[2,64,71,512]{3,2,1,0:T(8,128)(2,1)} %copy_dynamic-u, ...), kind=kLoop, calls=%fused_computation.106 | loop fusion | bytes 117440512 | tf_op jit(solution)/shard_map/slice | solution.py:68
  313.6 8.4 %convolution_add_fusion.6 = f32[8192,256]{1,0:T(8,128)S(1)} fusion(f32[8192,256]{1,0:T(8,128)} %fusion.113, bf16[8192,512]{1,0:T(8,128)(2,1)} %bitcast.78, s32[512,256]{1,0:T(8,128)S(1)} %copy-done), kind=kOutput, calls=%fused_computation.8 | convolution fusion | flops 2149711872 | bytes 25690112 | tf_op jit(solution)/shard_map/dot_general | solution.py:75
  322.0 6.1 %convolution_add_fusion.5 = f32[8192,256]{1,0:T(8,128)S(1)} fusion(f32[8192,256]{1,0:T(8,128)S(1)} %convolution_add_fusion.6, bf16[8192,512]{1,0:T(8,128)(2,1)} %bitcast.77, s32[512,256]{1,0:T(8,128)S(1)} %copy-done), kind=kOutput, calls=%fused_computation.7 | convolution fusion | flops 2149711872 | bytes 25690112 | tf_op jit(solution)/shard_map/dot_general | solution.py:75
  328.1 6.1 %convolution_add_fusion.4 = f32[8192,256]{1,0:T(8,128)S(1)} fusion(f32[8192,256]{1,0:T(8,128)S(1)} %convolution_add_fusion.5, bf16[8192,512]{1,0:T(8,128)(2,1)} %bitcast.76, s32[512,256]{1,0:T(8,128)S(1)} %copy-done), kind=kOutput, calls=%fused_computation.6 | convolution fusion | flops 2149711872 | bytes 25690112 | tf_op jit(solution)/shard_map/dot_general | solution.py:75
  336.7 6.3 %convolution_add_fusion.2 = f32[8192,256]{1,0:T(8,128)S(1)} fusion(f32[8192,256]{1,0:T(8,128)S(1)} %convolution_add_fusion.3, bf16[8192,512]{1,0:T(8,128)(2,1)} %bitcast.72, s32[512,256]{1,0:T(8,128)S(1)} %copy-done), kind=kOutput, calls=%fused_computation.4 | convolution fusion | flops 2149711872 | bytes 25690112 | tf_op jit(solution)/shard_map/dot_general | solution.py:75
  343.0 6.0 %convolution_add_fusion.1 = f32[8192,256]{1,0:T(8,128)S(1)} fusion(f32[8192,256]{1,0:T(8,128)S(1)} %convolution_add_fusion.2, bf16[8192,512]{1,0:T(8,128)(2,1)} %bitcast.71, s32[512,256]{1,0:T(8,128)S(1)} %copy-done), kind=kOutput, calls=%fused_computation.3 | convolution fusion | flops 2149711872 | bytes 25690112 | tf_op jit(solution)/shard_map/dot_general | solution.py:75
  349.0 9.2 %fusion = f32[8192,256]{1,0:T(8,128)} fusion(f32[8192,256]{1,0:T(8,128)S(1)} %convolution_add_fusion.1, bf16[8192,512]{1,0:T(8,128)(2,1)} %bitcast.70, s32[512,256]{1,0:T(8,128)S(1)} %copy-done), kind=kOutput, calls=%fused_computation.2 | convolution fusion | flops 2151809024 | bytes 25690112 | tf_op jit(solution)/shard_map/dot_general | solution.py:75
  358.2 39.2 %all-reduce.3.cloned.1.call-done = f32[8192,256]{1,0:T(8,128)} async-done(((f32[8192,256]{1,0:T(8,128)}), f32[8192,256]{1,0:T(8,128)}) %all-reduce.3.cloned.1.call-update) | async-done | bytes 8388624 | tf_op jit(solution)/shard_map/psum | solution.py:78
  (47 shorter events, 38.5 us)
Async XLA Ops:
  7.6 68.9 %collective-permute-start = (bf16[511,512]{1,0:T(8,128)(2,1)S(1)}, bf16[511,512]{1,0:T(8,128)(2,1)S(1)}, u32[]{:S(2)}, u32[]{:S(2)}) collective-permute-start(bf16[511,512]{1,0:T(8,128)(2,1)S(1)} %slice.73), channel_id=1, source_target_pairs={{2,0},{4,2},{6,4},{8,6},{10,8},{12,10},{14,12},{3,1},{5,3},{7,5},{... | collective-permute-start | bytes 1569800 | tf_op jit(solution)/shard_map/ppermute | solution.py:18
  40.9 7.3 %copy-start.1 = (bf16[512,4606]{1,0:T(8,128)(2,1)S(1)}, bf16[512,4606]{1,0:T(8,128)(2,1)}, u32[]{:S(2)}) copy-start(bf16[512,4606]{1,0:T(8,128)(2,1)} %convert_element_type.50) | copy-start | bytes 14149636
  48.2 12.6 %slice-start.2 = ((s8[33546240]{0:T(1024)(128)(4,1)}), s8[4194304]{0:T(1024)(128)(4,1)S(1)}, s32[]{:S(2)}) async-start(s8[33546240]{0:T(1024)(128)(4,1)} %bitcast.81), calls=%async_computation.4 | async-start | bytes 8388608
  48.2 12.6 %slice-start.3 = ((s8[33546240]{0:T(1024)(128)(4,1)}), s8[4194304]{0:T(1024)(128)(4,1)S(1)}, s32[]{:S(2)}) async-start(s8[33546240]{0:T(1024)(128)(4,1)} %bitcast.81), calls=%async_computation.5 | async-start | bytes 8388608
  48.2 12.6 %slice-start.4 = ((s8[33546240]{0:T(1024)(128)(4,1)}), s8[4194304]{0:T(1024)(128)(4,1)S(1)}, s32[]{:S(2)}) async-start(s8[33546240]{0:T(1024)(128)(4,1)} %bitcast.81), calls=%async_computation.6 | async-start | bytes 8388608
  48.3 12.6 %slice-start.5 = ((s8[33546240]{0:T(1024)(128)(4,1)}), s8[4194304]{0:T(1024)(128)(4,1)S(1)}, s32[]{:S(2)}) async-start(s8[33546240]{0:T(1024)(128)(4,1)} %bitcast.81), calls=%async_computation.7 | async-start | bytes 8388608
  48.3 12.6 %slice-start.6 = ((s8[33546240]{0:T(1024)(128)(4,1)}), s8[4194304]{0:T(1024)(128)(4,1)S(1)}, s32[]{:S(2)}) async-start(s8[33546240]{0:T(1024)(128)(4,1)} %bitcast.81), calls=%async_computation.8 | async-start | bytes 8388608
  54.2 6.6 %slice-start.7 = ((s8[33546240]{0:T(1024)(128)(4,1)}), s8[4194304]{0:T(1024)(128)(4,1)S(1)}, s32[]{:S(2)}) async-start(s8[33546240]{0:T(1024)(128)(4,1)} %bitcast.81), calls=%async_computation.9 | async-start | bytes 8388608
  54.2 6.7 %slice-start.8 = ((s8[33546240]{0:T(1024)(128)(4,1)}), s8[4194304]{0:T(1024)(128)(4,1)S(1)}, s32[]{:S(2)}) async-start(s8[33546240]{0:T(1024)(128)(4,1)} %bitcast.81), calls=%async_computation.10 | async-start | bytes 8388608
  54.2 8.0 %slice-start.9 = ((s8[33546240]{0:T(1024)(128)(4,1)}), s8[4186112]{0:T(1024)(128)(4,1)S(1)}, s32[]{:S(2)}) async-start(s8[33546240]{0:T(1024)(128)(4,1)} %bitcast.81), calls=%async_computation.11 | async-start | bytes 8372224
  89.3 101.4 %all-to-all-start = ((bf16[8,512,512]{2,0,1:T(8,128)(2,1)}), bf16[8,512,512]{2,0,1:T(8,128)(2,1)}, u32[]{:S(2)}, u32[]{:S(2)}) async-start(bf16[8,512,512]{2,0,1:T(8,128)(2,1)} %copy.5), calls=%async_computation | async-start | bytes 8388608 | tf_op jit(solution)/shard_map/all_to_all | solution.py:57
  97.8 299.7 %all-reduce.3.cloned.1.call-start = ((), (), s32[]{:S(2)}) async-start(), calls=%async_computation.1 | async-start | bytes 16777216 | tf_op jit(solution)/shard_map/psum | solution.py:78
  226.6 10.9 %copy-start = (s32[512,256]{1,0:T(8,128)S(1)}, s32[512,256]{1,0:T(8,128)}, u32[]{:S(2)}) copy-start(s32[512,256]{1,0:T(8,128)} %param.5) | copy-start | bytes 1572868
  236.2 22.9 %collective-permute-start.1 = (bf16[2,64,7,512]{3,1,2,0:T(8,128)(2,1)S(1)}, bf16[2,64,7,512]{3,1,2,0:T(8,128)(2,1)S(1)}, u32[]{:S(2)}, u32[]{:S(2)}) collective-permute-start(bf16[2,64,7,512]{3,1,2,0:T(8,128)(2,1)S(1)} %copy.9), channel_id=1, source_target_pairs={{2,0},{4,2},{6,4},{8,6},{10,8},{12,10},{14,12},{3,1},{5,3},{7,5},{... | collective-permute-start | bytes 2752520 | tf_op jit(solution)/shard_map/ppermute | solution.py:18
  322.0 12.3 %slice-start = ((s8[8388608]{0:T(1024)(128)(4,1)}), s8[4194304]{0:T(1024)(128)(4,1)S(1)}, s32[]{:S(2)}) async-start(s8[8388608]{0:T(1024)(128)(4,1)} %bitcast.73), calls=%async_computation.2 | async-start | bytes 8388608
  328.1 6.2 %slice-start.1 = ((s8[8388608]{0:T(1024)(128)(4,1)}), s8[4194304]{0:T(1024)(128)(4,1)S(1)}, s32[]{:S(2)}) async-start(s8[8388608]{0:T(1024)(128)(4,1)} %bitcast.73), calls=%async_computation.3 | async-start | bytes 8388608
Sparse Core Ops, SparseCore 0:
  358.3 39.0 all-reduce.2
where the time goes:
time: 416 us; the launch traced here: 409 us
  waiting for transfers between devices  145 us (35%)
  local copies, waits for them, and re-layouts  135 us (32%)
  matrix products  99.3 us (24%)
  between operations  14.1 us (3%)
  starting transfers between devices  11 us (3%)
  other arithmetic  4.64 us (1%)
    all_to_all x1, waiting for transfers between devices, body(): lax.all_to_all(profiles, 'tm', split_axis=1, concat_axis=0, tiled=True)  92.8 us
    dot_general x8, matrix products, body(): jnp.dot(shifted_list[offset], selector, preferred_element_type=jnp.float32)  53.7 us
    slice x1, local copies, waits for them, and re-layouts, body(): spec_ext[:, :, offset:offset + delay_rows, :]  52.8 us
    dot_general x8, matrix products, body(): jnp.dot(toeplitz, segment, preferred_element_type=jnp.float32) * norm_code  40 us
    psum x1, waiting for transfers between devices, body(): summed = lax.psum(partial_sum * norm_hydro, 'hyd')  39.2 us
    unnamed x28, local copies, waits for them, and re-layouts  22.6 us
    another operation x2, local copies, waits for them, and re-layouts, toeplitz_code(): tiled = jnp.tile(padded, DELAYS)[:DELAYS * seg_len]  14.3 us
    another operation x1, local copies, waits for them, and re-layouts, body(): spec_ext[:, :, offset:offset + delay_rows, :]  13.6 us
  transfers between devices with their start and end apart: 4, of which 3 were waited for; matrix products, arithmetic and copies ran while one was open for 18% of the time, Pallas kernels for 0%

commit v1 on v0

--- a/solution.py
+++ b/solution.py
@@ -75,7 +75,7 @@
         partial_sum = partial_sum + jnp.dot(
             shifted_list[offset], selector, preferred_element_type=jnp.float32
         )
-    summed = lax.psum(partial_sum * norm_hydro, "hyd")
+    summed = jnp.sum(lax.all_gather(partial_sum * norm_hydro, "hyd"), axis=0)
     owned = lax.dynamic_slice_in_dim(summed, lax.axis_index("hyd") * beam_local, beam_local, 1)
     owned = owned.reshape(2, PERIODS, delay_rows, beam_local)
     return owned[0] * owned[0] + owned[1] * owned[1]

time: 416 us -> 418 us (level)
  other arithmetic: 4.64 us -> 15.9 us
  waiting for transfers between devices: 145 us -> 136 us
    psum x1 -> x0, waiting for transfers between devices: 39.2 us -> none  [body(): summed = lax.psum(partial_sum * norm_hydro, 'hyd')]
    all_gather x0 -> x1, waiting for transfers between devices: none -> 30.4 us  [body(): summed = jnp.sum(lax.all_gather(partial_sum * norm_hydro, 'hyd'), axis=0)]
    reduce_sum x0 -> x1, other arithmetic: none -> 11.3 us  [body(): summed = jnp.sum(lax.all_gather(partial_sum * norm_hydro, 'hyd'), axis=0)]
where the time goes in v1:
time: 418 us; the launch traced here: 411 us
  waiting for transfers between devices  136 us (33%)
  local copies, waits for them, and re-layouts  135 us (32%)
  matrix products  99.3 us (24%)
  other arithmetic  15.9 us (4%)
  between operations  14.1 us (3%)
  starting transfers between devices  11 us (3%)
    all_to_all x1, waiting for transfers between devices, body(): lax.all_to_all(profiles, 'tm', split_axis=1, concat_axis=0, tiled=True)  92.8 us
    dot_general x8, matrix products, body(): jnp.dot(shifted_list[offset], selector, preferred_element_type=jnp.float32)  53.6 us
    slice x1, local copies, waits for them, and re-layouts, body(): spec_ext[:, :, offset:offset + delay_rows, :]  52.8 us
    dot_general x8, matrix products, body(): jnp.dot(toeplitz, segment, preferred_element_type=jnp.float32) * norm_code  40 us
    all_gather x1, waiting for transfers between devices, body(): summed = jnp.sum(lax.all_gather(partial_sum * norm_hydro, 'hyd'), axis=0)  30.4 us
    unnamed x28, local copies, waits for them, and re-layouts  22.6 us
    another operation x2, local copies, waits for them, and re-layouts, toeplitz_code(): tiled = jnp.tile(padded, DELAYS)[:DELAYS * seg_len]  14.3 us
    another operation x1, local copies, waits for them, and re-layouts, body(): spec_ext[:, :, offset:offset + delay_rows, :]  13.6 us
  transfers between devices with their start and end apart: 4, of which 3 were waited for; matrix products, arithmetic and copies ran while one was open for 18% of the time, Pallas kernels for 0%

profile of v1, /device:TPU:0, one launch (start us, length us, event | category | flops | bytes accessed | tf_op | source)
XLA Modules:
  0.0 411.1 jit_solution(8085662283641363496)
XLA Ops:
  12.1 11.8 %tile.11 = bf16[2358784]{0:T(1024)(128)(2,1)} reshape(bf16[512,4607]{1,0:T(8,128)(2,1)} %tile.10) | data formatting | bytes 9435136 | tf_op jit(solution)/shard_map/tile | solution.py:24
  23.9 5.7 %slice.85 = bf16[2358272]{0:T(1024)(128)(2,1)} slice(bf16[2358784]{0:T(1024)(128)(2,1)} %tile.11), slice={[0:2358272]} | slice | bytes 9433088 | tf_op jit(solution)/shard_map/slice | solution.py:24
  29.6 11.3 %convert_element_type.50 = bf16[512,4606]{1,0:T(8,128)(2,1)} reshape(bf16[2358272]{0:T(1024)(128)(2,1)} %slice.85) | data formatting | bytes 9433088 | tf_op jit(solution)/shard_map/convert_element_type | solution.py:25
  40.9 7.3 %fusion.65 = bf16[8,512,512]{2,1,0:T(8,128)(2,1)} fusion(bf16[512,4606]{1,0:T(8,128)(2,1)} %convert_element_type.50, bf16[32760,512]{1,0:T(8,128)(2,1)} %param.3), kind=kOutput, calls=%fused_computation.47 | convolution fusion | flops 2415394816 | bytes 9961472 | tf_op jit(solution)/shard_map/dot_general | solution.py:51
  48.3 5.9 %fusion.73 = bf16[8,512,512]{2,1,0:T(8,128)(2,1)} fusion(bf16[8,512,512]{2,1,0:T(8,128)(2,1)} %fusion.65, bf16[512,4606]{1,0:T(8,128)(2,1)S(1)} %copy-done.1, bf16[32760,512]{1,0:T(8,128)(2,1)} %param.3), kind=kOutput, calls=%fused_computation.51 | convolution fusion | flops 2415394816 | bytes 9959424 | tf_op jit(solution)/shard_map/dot_general | solution.py:51
  54.2 6.6 %fusion.79 = bf16[8,512,512]{2,1,0:T(8,128)(2,1)} fusion(bf16[8,512,512]{2,1,0:T(8,128)(2,1)} %fusion.73, bf16[512,4606]{1,0:T(8,128)(2,1)S(1)} %copy-done.1, bf16[32760,512]{1,0:T(8,128)(2,1)} %param.3), kind=kOutput, calls=%fused_computation.53 | convolution fusion | flops 2415394816 | bytes 9959424 | tf_op jit(solution)/shard_map/dot_general | solution.py:51
  76.5 5.9 %fusion.69 = bf16[8,512,512]{2,1,0:T(8,128)(2,1)} fusion(bf16[8,512,512]{2,1,0:T(8,128)(2,1)} %fusion.103, bf16[512,4606]{1,0:T(8,128)(2,1)} %convert_element_type.50, bf16[511,512]{1,0:T(8,128)(2,1)S(1)} %collective-permute-done, bf16[32760,512]{1,0:T(8,128)(2,1)S(1)} %bitcast.83), kind=kOutput, calls=%fused_computation.49 | convolution fusion | flops 2424827904 | bytes 39312384 | tf_op jit(solution)/shard_map/dot_general | solution.py:51
  82.5 6.9 %copy.5 = bf16[8,512,512]{2,0,1:T(8,128)(2,1)} copy(bf16[8,512,512]{2,1,0:T(8,128)(2,1)} %fusion.69) | data formatting | bytes 8388608 | tf_op jit(solution)/shard_map/stack | solution.py:55
  89.3 8.4 %all-to-all-start = ((bf16[8,512,512]{2,0,1:T(8,128)(2,1)}), bf16[8,512,512]{2,0,1:T(8,128)(2,1)}, u32[]{:S(2)}, u32[]{:S(2)}) async-start(bf16[8,512,512]{2,0,1:T(8,128)(2,1)} %copy.5), calls=%async_computation | async-start | bytes 8388608 | tf_op jit(solution)/shard_map/all_to_all | solution.py:57
  98.0 92.8 %all-to-all-done = bf16[8,512,512]{2,0,1:T(8,128)(2,1)} async-done(((bf16[8,512,512]{2,0,1:T(8,128)(2,1)}), bf16[8,512,512]{2,0,1:T(8,128)(2,1)}, u32[]{:S(2)}, u32[]{:S(2)}) %all-to-all-start) | async-done | bytes 4194336 | tf_op jit(solution)/shard_map/all_to_all | solution.py:57
  202.7 13.6 %reshape_reshape.3 = bf16[8192,512]{1,0:T(8,128)(2,1)} reshape(bf16[128,32768]{1,0:T(8,128)(2,1)} %convolution_convert_fusion) | data formatting | bytes 16777216 | tf_op jit(solution)/shard_map/reshape;reshape | solution.py:68
  216.3 10.2 %copy.11 = bf16[16,8,64,512]{3,2,1,0:T(8,128)(2,1)} copy(bf16[16,8,64,512]{3,1,2,0:T(8,128)(2,1)} %bitcast.70) | data formatting | bytes 16777216
  226.6 8.0 %constant_dynamic-update-slice_fusion = bf16[2,64,71,512]{3,2,1,0:T(8,128)(2,1)} fusion(bf16[2,64,64,512]{3,2,1,0:T(8,128)(2,1)} %bitcast.80), kind=kLoop, calls=%fused_computation.94 | loop fusion | bytes 16777216
  237.5 9.1 %fusion.113 = f32[8192,256]{1,0:T(8,128)} fusion(bf16[8192,512]{1,0:T(8,128)(2,1)} %reshape_reshape.3, s32[512,256]{1,0:T(8,128)S(1)} %copy-done), kind=kOutput, calls=%fused_computation.70 | convolution fusion | flops 2147614720 | bytes 17301504 | tf_op jit(solution)/shard_map/dot_general | solution.py:75
  246.7 12.5 %collective-permute-done.1 = bf16[2,64,7,512]{3,1,2,0:T(8,128)(2,1)S(1)} collective-permute-done((bf16[2,64,7,512]{3,1,2,0:T(8,128)(2,1)S(1)}, bf16[2,64,7,512]{3,1,2,0:T(8,128)(2,1)S(1)}, u32[]{:S(2)}, u32[]{:S(2)}) %collective-permute-start.1) | collective-permute-done | bytes 917536 | tf_op jit(solution)/shard_map/ppermute | solution.py:18
  260.7 52.8 %fusion.142 = (bf16[2,64,64,512]{3,2,1,0:T(8,128)(2,1)}, bf16[2,64,64,512]{3,2,1,0:T(8,128)(2,1)}, bf16[2,64,64,512]{3,2,1,0:T(8,128)(2,1)}, bf16[2,64,64,512]{3...) fusion(bf16[2,64,71,512]{3,2,1,0:T(8,128)(2,1)} %copy_dynamic-u, ...), kind=kLoop, calls=%fused_computation.106 | loop fusion | bytes 117440512 | tf_op jit(solution)/shard_map/slice | solution.py:68
  313.6 8.4 %convolution_add_fusion.6 = f32[8192,256]{1,0:T(8,128)S(1)} fusion(f32[8192,256]{1,0:T(8,128)} %fusion.113, bf16[8192,512]{1,0:T(8,128)(2,1)} %bitcast.79, s32[512,256]{1,0:T(8,128)S(1)} %copy-done), kind=kOutput, calls=%fused_computation.8 | convolution fusion | flops 2149711872 | bytes 25690112 | tf_op jit(solution)/shard_map/dot_general | solution.py:75
  322.0 6.1 %convolution_add_fusion.5 = f32[8192,256]{1,0:T(8,128)S(1)} fusion(f32[8192,256]{1,0:T(8,128)S(1)} %convolution_add_fusion.6, bf16[8192,512]{1,0:T(8,128)(2,1)} %bitcast.78, s32[512,256]{1,0:T(8,128)S(1)} %copy-done), kind=kOutput, calls=%fused_computation.7 | convolution fusion | flops 2149711872 | bytes 25690112 | tf_op jit(solution)/shard_map/dot_general | solution.py:75
  328.1 6.1 %convolution_add_fusion.4 = f32[8192,256]{1,0:T(8,128)S(1)} fusion(f32[8192,256]{1,0:T(8,128)S(1)} %convolution_add_fusion.5, bf16[8192,512]{1,0:T(8,128)(2,1)} %bitcast.77, s32[512,256]{1,0:T(8,128)S(1)} %copy-done), kind=kOutput, calls=%fused_computation.6 | convolution fusion | flops 2149711872 | bytes 25690112 | tf_op jit(solution)/shard_map/dot_general | solution.py:75
  336.7 6.3 %convolution_add_fusion.2 = f32[8192,256]{1,0:T(8,128)S(1)} fusion(f32[8192,256]{1,0:T(8,128)S(1)} %convolution_add_fusion.3, bf16[8192,512]{1,0:T(8,128)(2,1)} %bitcast.73, s32[512,256]{1,0:T(8,128)S(1)} %copy-done), kind=kOutput, calls=%fused_computation.4 | convolution fusion | flops 2149711872 | bytes 25690112 | tf_op jit(solution)/shard_map/dot_general | solution.py:75
  343.0 6.0 %convolution_add_fusion.1 = f32[8192,256]{1,0:T(8,128)S(1)} fusion(f32[8192,256]{1,0:T(8,128)S(1)} %convolution_add_fusion.2, bf16[8192,512]{1,0:T(8,128)(2,1)} %bitcast.72, s32[512,256]{1,0:T(8,128)S(1)} %copy-done), kind=kOutput, calls=%fused_computation.3 | convolution fusion | flops 2149711872 | bytes 25690112 | tf_op jit(solution)/shard_map/dot_general | solution.py:75
  349.0 9.1 %fusion = f32[8192,256]{1,0:T(8,128)} fusion(f32[8192,256]{1,0:T(8,128)S(1)} %convolution_add_fusion.1, bf16[8192,512]{1,0:T(8,128)(2,1)} %bitcast.71, s32[512,256]{1,0:T(8,128)S(1)} %copy-done), kind=kOutput, calls=%fused_computation.2 | convolution fusion | flops 2151809024 | bytes 25690112 | tf_op jit(solution)/shard_map/dot_general | solution.py:75
  358.2 30.4 %all-gather.3.cloned.1.call-done = f32[16384,256]{1,0:T(8,128)} async-done(((f32[8192,256]{1,0:T(8,128)}), f32[16384,256]{1,0:T(8,128)}) %all-gather.3.cloned.1.call-update) | async-done | bytes 16777232 | tf_op jit(solution)/shard_map/all_gather | solution.py:78
  388.6 11.3 %reduce_sum.9 = f32[8192,256]{1,0:T(8,128)} reduce(f32[2,8192,256]{2,1,0:T(8,128)} %bitcast.85, f32[]{:T(128)} %constant.9.clone.1), dimensions={0}, to_apply=%region_0.1 | reduce | flops 2097152 | bytes 25165828 | tf_op jit(solution)/shard_map/reduce_sum | solution.py:78
  (48 shorter events, 44.1 us)
Async XLA Ops:
  7.6 68.9 %collective-permute-start = (bf16[511,512]{1,0:T(8,128)(2,1)S(1)}, bf16[511,512]{1,0:T(8,128)(2,1)S(1)}, u32[]{:S(2)}, u32[]{:S(2)}) collective-permute-start(bf16[511,512]{1,0:T(8,128)(2,1)S(1)} %slice.73), channel_id=1, source_target_pairs={{2,0},{4,2},{6,4},{8,6},{10,8},{12,10},{14,12},{3,1},{5,3},{7,5},{... | collective-permute-start | bytes 1569800 | tf_op jit(solution)/shard_map/ppermute | solution.py:18
  40.9 7.3 %copy-start.1 = (bf16[512,4606]{1,0:T(8,128)(2,1)S(1)}, bf16[512,4606]{1,0:T(8,128)(2,1)}, u32[]{:S(2)}) copy-start(bf16[512,4606]{1,0:T(8,128)(2,1)} %convert_element_type.50) | copy-start | bytes 14149636
  48.2 12.6 %slice-start.2 = ((s8[33546240]{0:T(1024)(128)(4,1)}), s8[4194304]{0:T(1024)(128)(4,1)S(1)}, s32[]{:S(2)}) async-start(s8[33546240]{0:T(1024)(128)(4,1)} %bitcast.82), calls=%async_computation.4 | async-start | bytes 8388608
  48.2 12.6 %slice-start.3 = ((s8[33546240]{0:T(1024)(128)(4,1)}), s8[4194304]{0:T(1024)(128)(4,1)S(1)}, s32[]{:S(2)}) async-start(s8[33546240]{0:T(1024)(128)(4,1)} %bitcast.82), calls=%async_computation.5 | async-start | bytes 8388608
  48.2 12.6 %slice-start.4 = ((s8[33546240]{0:T(1024)(128)(4,1)}), s8[4194304]{0:T(1024)(128)(4,1)S(1)}, s32[]{:S(2)}) async-start(s8[33546240]{0:T(1024)(128)(4,1)} %bitcast.82), calls=%async_computation.6 | async-start | bytes 8388608
  48.3 12.6 %slice-start.5 = ((s8[33546240]{0:T(1024)(128)(4,1)}), s8[4194304]{0:T(1024)(128)(4,1)S(1)}, s32[]{:S(2)}) async-start(s8[33546240]{0:T(1024)(128)(4,1)} %bitcast.82), calls=%async_computation.7 | async-start | bytes 8388608
  48.3 12.6 %slice-start.6 = ((s8[33546240]{0:T(1024)(128)(4,1)}), s8[4194304]{0:T(1024)(128)(4,1)S(1)}, s32[]{:S(2)}) async-start(s8[33546240]{0:T(1024)(128)(4,1)} %bitcast.82), calls=%async_computation.8 | async-start | bytes 8388608
  54.2 6.6 %slice-start.7 = ((s8[33546240]{0:T(1024)(128)(4,1)}), s8[4194304]{0:T(1024)(128)(4,1)S(1)}, s32[]{:S(2)}) async-start(s8[33546240]{0:T(1024)(128)(4,1)} %bitcast.82), calls=%async_computation.9 | async-start | bytes 8388608
  54.2 6.7 %slice-start.8 = ((s8[33546240]{0:T(1024)(128)(4,1)}), s8[4194304]{0:T(1024)(128)(4,1)S(1)}, s32[]{:S(2)}) async-start(s8[33546240]{0:T(1024)(128)(4,1)} %bitcast.82), calls=%async_computation.10 | async-start | bytes 8388608
  54.2 8.0 %slice-start.9 = ((s8[33546240]{0:T(1024)(128)(4,1)}), s8[4186112]{0:T(1024)(128)(4,1)S(1)}, s32[]{:S(2)}) async-start(s8[33546240]{0:T(1024)(128)(4,1)} %bitcast.82), calls=%async_computation.11 | async-start | bytes 8372224
  89.3 101.4 %all-to-all-start = ((bf16[8,512,512]{2,0,1:T(8,128)(2,1)}), bf16[8,512,512]{2,0,1:T(8,128)(2,1)}, u32[]{:S(2)}, u32[]{:S(2)}) async-start(bf16[8,512,512]{2,0,1:T(8,128)(2,1)} %copy.5), calls=%async_computation | async-start | bytes 8388608 | tf_op jit(solution)/shard_map/all_to_all | solution.py:57
  97.8 290.9 %all-gather.3.cloned.1.call-start = ((), (), s32[]{:S(2)}) async-start(), calls=%async_computation.1 | async-start | bytes 25165824 | tf_op jit(solution)/shard_map/all_gather | solution.py:78
  226.6 10.9 %copy-start = (s32[512,256]{1,0:T(8,128)S(1)}, s32[512,256]{1,0:T(8,128)}, u32[]{:S(2)}) copy-start(s32[512,256]{1,0:T(8,128)} %param.5) | copy-start | bytes 1572868
  236.2 22.9 %collective-permute-start.1 = (bf16[2,64,7,512]{3,1,2,0:T(8,128)(2,1)S(1)}, bf16[2,64,7,512]{3,1,2,0:T(8,128)(2,1)S(1)}, u32[]{:S(2)}, u32[]{:S(2)}) collective-permute-start(bf16[2,64,7,512]{3,1,2,0:T(8,128)(2,1)S(1)} %copy.9), channel_id=1, source_target_pairs={{2,0},{4,2},{6,4},{8,6},{10,8},{12,10},{14,12},{3,1},{5,3},{7,5},{... | collective-permute-start | bytes 2752520 | tf_op jit(solution)/shard_map/ppermute | solution.py:18
  322.0 12.3 %slice-start = ((s8[8388608]{0:T(1024)(128)(4,1)}), s8[4194304]{0:T(1024)(128)(4,1)S(1)}, s32[]{:S(2)}) async-start(s8[8388608]{0:T(1024)(128)(4,1)} %bitcast.74), calls=%async_computation.2 | async-start | bytes 8388608
  328.1 6.2 %slice-start.1 = ((s8[8388608]{0:T(1024)(128)(4,1)}), s8[4194304]{0:T(1024)(128)(4,1)S(1)}, s32[]{:S(2)}) async-start(s8[8388608]{0:T(1024)(128)(4,1)} %bitcast.74), calls=%async_computation.3 | async-start | bytes 8388608
Sparse Core Ops, SparseCore 0:
  358.3 30.2 all-gather.2
